TPU v7x, 512 devices: a whole 4x4x16 slice. The times are simulated.
512 devices in a mesh: mem: 16 (over y, x), tile: 32 (over z, core).
Axes of the slice: x: 4, y: 4, z: 16, core: 2. Of those that a mesh axis runs over, the one named last changes fastest.
Arguments:
- state: float32 [256, 2048, 4, 128], P('mem', 'tile'), may hold values from -6 to 6
- obs_prior: float32 [256, 2048, 128], P('mem', 'tile'), may hold values from -6 to 6
- obs_value: float32 [2048, 128], P('tile'), may hold values from -6 to 6
- obs_prec: float32 [2048, 128], P('tile'), may hold values from 0.05 to 1
- tile_batches: int32 [2048, 6], P('tile'), may hold values from 0 to 2047, as said below
- tile_count: int32 [2048], P('tile'), may hold values from 1 to 6, as said below
- loc_weight: float32 [2048, 6], P('tile'), may hold values from 0.1 to 1
Outputs:
- analysis: float32 [256, 2048, 4, 128], P('mem', 'tile')
Inputs may be any that keep to these rules, and one draw needn't show every extreme that they name: `tile_batches`: row t holds 6 different batch numbers (t + o) mod 2048 with |o| <= 16. Only the first tile_count[t] entries of row t of tile_batches and loc_weight are used.
All inputs are finite; a program needn't handle non-finite values.
Results may differ from a plain program's by a relative error of at most 0.0003.
Values sent between devices are 32-bit elements; how exact they have to be, the bound alone decides.
A program may use at most 128 MiB of HBM per device.

v0:
```python
import jax
import jax.numpy as jnp
from jax import lax
from jax.sharding import PartitionSpec as P

SWEEPS = 3


def extended(cells, sides, width):
    for axis, dim in sides:
        count = lax.axis_size(axis)
        head = lax.slice_in_dim(cells, 0, width, axis=dim)
        tail = lax.slice_in_dim(cells, cells.shape[dim] - width, cells.shape[dim], axis=dim)
        cells = jnp.concatenate(
            [
                lax.ppermute(tail, axis, [(i, (i + 1) % count) for i in range(count)]),
                cells,
                lax.ppermute(head, axis, [((i + 1) % count, i) for i in range(count)]),
            ],
            axis=dim,
        )
    return cells


def finish(xmean, xpert, gram, proj):
    highest = lax.Precision.HIGHEST
    members = xpert.shape[0]
    ident = jnp.eye(members, dtype=jnp.float32)
    amat = (members - 1.0) * ident + gram
    scale = jnp.sqrt(jnp.sum(amat * amat))
    root = amat / scale
    inverse = ident
    for sweep in range(SWEEPS):
        factor = 1.5 * ident - 0.5 * jnp.dot(inverse, root, precision=highest)
        root = jnp.dot(root, factor, precision=highest)
        inverse = jnp.dot(factor, inverse, precision=highest)
    cover = jnp.dot(inverse, inverse, precision=highest) / scale
    wmean = jnp.dot(cover, proj, precision=highest)
    weights = jnp.sqrt((members - 1.0) / scale) * inverse + wmean[:, None]
    flat = xpert.reshape(members, -1)
    moved = jnp.dot(weights.T, flat, precision=highest)
    return xmean + moved.reshape(xpert.shape)


def update_tile(tile_state, prior, values, precs, weight, count):
    highest = lax.Precision.HIGHEST
    members = tile_state.shape[0]
    xmean = jnp.mean(tile_state, axis=0)
    xpert = tile_state - xmean
    ymean = jnp.mean(prior, axis=0)
    ypert = prior - ymean
    innov = values - ymean
    scaled = ypert * (precs * weight[:, None])

    def add_slot(slot, carry):
        gram, proj = carry
        left = lax.dynamic_index_in_dim(scaled, slot, 1, False)
        right = lax.dynamic_index_in_dim(ypert, slot, 1, False)
        misfit = lax.dynamic_index_in_dim(innov, slot, 0, False)
        gram = gram + jnp.dot(left, right.T, precision=highest)
        proj = proj + jnp.dot(left, misfit, precision=highest)
        return (gram, proj)

    start = (jnp.zeros((members, members), jnp.float32), jnp.zeros((members,), jnp.float32))
    gram, proj = lax.fori_loop(0, count, add_slot, start)
    return finish(xmean, xpert, gram, proj)


def per_device(state, obs_prior, obs_value, obs_prec, tile_batches, tile_count, loc_weight):
    mem_count = lax.axis_size("mem")
    mem_index = lax.axis_index("mem")
    tile_index = lax.axis_index("tile")
    tiles_shard = state.shape[1]
    tiles_here = tiles_shard // mem_count
    local_members = obs_prior.shape[0]
    total_batches = obs_value.shape[0] * lax.axis_size("tile")
    reach = tiles_shard // 4
    first_tile = mem_index * tiles_here
    complete = lax.all_to_all(state, "mem", split_axis=1, concat_axis=0, tiled=True)
    stacked = jnp.concatenate([obs_prior, obs_value[None], obs_prec[None]], axis=0)
    rimmed = extended(stacked, (("tile", 1),), reach)
    prior_rim = rimmed[:local_members]
    extra_rim = rimmed[local_members:]
    listed = lax.dynamic_slice_in_dim(tile_batches, first_tile, tiles_here, 0)
    counts = lax.dynamic_slice_in_dim(tile_count, first_tile, tiles_here, 0)
    weights = lax.dynamic_slice_in_dim(loc_weight, first_tile, tiles_here, 0)
    rim_base = tile_index * tiles_shard - reach
    prior_all = lax.all_gather(prior_rim, "mem", axis=0, tiled=True)
    positions = (listed - rim_base) % total_batches

    def run_tile(number):
        tile_state = lax.dynamic_index_in_dim(complete, number, 1, False)
        where_rows = positions[number]
        prior = jnp.take(prior_all, positions[number], axis=1)
        values = jnp.take(extra_rim[0], where_rows, axis=0)
        precs = jnp.take(extra_rim[1], where_rows, axis=0)
        return update_tile(tile_state, prior, values, precs, weights[number], counts[number])

    updated = lax.map(run_tile, jnp.arange(tiles_here, dtype=jnp.int32))
    updated = jnp.moveaxis(updated, 0, 1)
    return lax.all_to_all(updated, "mem", split_axis=0, concat_axis=1, tiled=True)


def solution(mesh):
    in_specs = (
        P("mem", "tile", None, None),
        P("mem", "tile", None),
        P("tile", None),
        P("tile", None),
        P("tile", None),
        P("tile"),
        P("tile", None),
    )
    out_specs = P("mem", "tile", None, None)
    return jax.shard_map(
        per_device, mesh=mesh, in_specs=in_specs, out_specs=out_specs, check_vma=False
    )
```

profile of v0, /device:TPU:6, one launch (start us, length us, event | category | flops | bytes accessed | tf_op | source)
XLA Modules:
  0.0 296.9 jit_solution(15731203136759775004)
XLA Ops:
  6.5 1.1 pad_maximum_fusion.3
  7.6 8.9 %collective-permute-start.1 = (f32[18,16,128]{2,1,0:T(8,128)S(1)}, f32[18,16,128]{2,1,0:T(8,128)S(1)}, u32[]{:S(2)}, u32[]{:S(2)}) collective-permute-start(f32[18,16,128]{2,1,0:T(8,128)S(1)} %get-tuple-element.187), channel_id=1, source_target_pairs={{1,0},{2,1},{3,2},{4,3},{5,4},{6,5},{7,6},{8,7},{9,8},{10,9},{11,1... | collective-permute-start | bytes 442376 | tf_op jit(solution)/shard_map/ppermute | solution.py:18
  16.6 2.8 collective-permute-done
  19.4 1.2 pad_maximum_fusion
  20.6 1.0 slice.28
  21.5 4.1 %copy.34 = f32[16,64,4,128]{3,0,2,1:T(8,128)} copy(f32[16,64,4,128]{3,2,1,0:T(4,128)} %param.13) | data formatting | bytes 4194304 | tf_op args[0]
  25.7 7.6 %all-to-all-start = ((f32[16,64,4,128]{3,0,2,1:T(8,128)}), f32[16,64,4,128]{3,0,2,1:T(8,128)S(1)}, u32[]{:S(2)}, u32[]{:S(2)}) async-start(f32[16,64,4,128]{3,0,2,1:T(8,128)} %copy.34), calls=%async_computation | async-start | bytes 4194304 | tf_op jit(solution)/shard_map/all_to_all | solution.py:79
  33.8 31.1 %all-to-all-done = f32[16,64,4,128]{3,0,2,1:T(8,128)S(1)} async-done(((f32[16,64,4,128]{3,0,2,1:T(8,128)}), f32[16,64,4,128]{3,0,2,1:T(8,128)S(1)}, u32[]{:S(2)}, u32[]{:S(2)}) %all-to-all-start) | async-done | bytes 2097184 | tf_op jit(solution)/shard_map/all_to_all | solution.py:79
  64.9 1.3 copy-done.3
  66.2 1.8 copy.35
  68.0 73.4 %all-gather.2.cloned.1.call-done = f32[256,96,128]{2,1,0:T(8,128)} async-done(((f32[16,96,128]{2,1,0:T(8,128)}), f32[256,96,128]{2,1,0:T(8,128)}) %all-gather.2.cloned.1.call-update) | async-done | bytes 12582928 | tf_op jit(solution)/shard_map/all_gather | solution.py:88
  141.4 16.4 %copy.39 = f32[256,96,128]{2,0,1:T(8,128)} copy(f32[256,96,128]{2,1,0:T(8,128)} %all-gather.2.cloned.1.call-done) | data formatting | bytes 25165824 | tf_op jit(solution)/shard_map/while | solution.py:99
  157.8 91.6 %while.23 = (s32[]{:T(128)}, f32[4,256,4,128]{3,2,0,1:T(4,128)}, s32[4]{0:T(128)S(1)}, f32[256,4,4,128]{3,0,2,1:T(8,128)S(1)}, s32[4]{0:T(128)S(1)}, /*index=5*/...) while((s32[]{:T(128)}, f32[4,256,4,128]{3,2,0,1:T(4,128)}, ...), condition=%wide.region_6.8_spmd, body=%wide.region_0.7_spmd.sunk | while | flops 2319848704 | bytes 35264896 | solution.py:99
  162.4 5.2 %gather_fusion.1 = f32[6,256,128]{2,1,0:T(8,128)S(1)} fusion(f32[256,96,128]{2,0,1:T(8,128)} %get-tuple-element.402, s32[1024]{0:T(1024)S(1)} %pad_clamp_fusion.5), kind=kCustom, calls=%fused_computation.2.clone.1 | custom fusion | bytes 1572888 | tf_op jit(solution)/shard_map/while/body/eval_jaxpr/jit(_take)/gather | solution.py:94
  168.0 8.3 %while.24 = (s32[]{:T(128)}, f32[256,256]{1,0:T(8,128)S(1)}, f32[256]{0:T(256)S(1)}, s32[]{:T(128)}, f32[256,6,128]{2,0,1:T(8,128)S(1)}, /*index=5*/f32[256,6,12...) while((s32[]{:T(128)}, f32[256,256]{1,0:T(8,128)S(1)}, f32[256]{0:T(256)S(1)}, ...), condition=%wide.region_4.5_spmd, body=%wide.region_3.4_spmd.sunk | while | flops 101122304 | bytes 924303 | solution.py:65
  176.3 0.7 multiply_reduce_fusion.2
  181.3 1.2 fusion.125
  182.5 1.1 copy_dynamic-update-slice_fusion.2
  188.2 5.2 %gather_fusion.1 = f32[6,256,128]{2,1,0:T(8,128)S(1)} fusion(f32[256,96,128]{2,0,1:T(8,128)} %get-tuple-element.402, s32[1024]{0:T(1024)S(1)} %pad_clamp_fusion.5), kind=kCustom, calls=%fused_computation.2.clone.1 | custom fusion | bytes 1572888 | tf_op jit(solution)/shard_map/while/body/eval_jaxpr/jit(_take)/gather | solution.py:94
  193.8 1.9 while.24
  200.7 1.2 fusion.125
  201.8 1.1 copy_dynamic-update-slice_fusion.2
  207.5 5.2 %gather_fusion.1 = f32[6,256,128]{2,1,0:T(8,128)S(1)} fusion(f32[256,96,128]{2,0,1:T(8,128)} %get-tuple-element.402, s32[1024]{0:T(1024)S(1)} %pad_clamp_fusion.5), kind=kCustom, calls=%fused_computation.2.clone.1 | custom fusion | bytes 1572888 | tf_op jit(solution)/shard_map/while/body/eval_jaxpr/jit(_take)/gather | solution.py:94
  213.2 7.0 %while.24 = (s32[]{:T(128)}, f32[256,256]{1,0:T(8,128)S(1)}, f32[256]{0:T(256)S(1)}, s32[]{:T(128)}, f32[256,6,128]{2,0,1:T(8,128)S(1)}, /*index=5*/f32[256,6,12...) while((s32[]{:T(128)}, f32[256,256]{1,0:T(8,128)S(1)}, f32[256]{0:T(256)S(1)}, ...), condition=%wide.region_4.5_spmd, body=%wide.region_3.4_spmd.sunk | while | flops 101122304 | bytes 924303 | solution.py:65
  225.2 1.2 fusion.125
  226.4 1.1 copy_dynamic-update-slice_fusion.2
  232.1 5.2 %gather_fusion.1 = f32[6,256,128]{2,1,0:T(8,128)S(1)} fusion(f32[256,96,128]{2,0,1:T(8,128)} %get-tuple-element.402, s32[1024]{0:T(1024)S(1)} %pad_clamp_fusion.5), kind=kCustom, calls=%fused_computation.2.clone.1 | custom fusion | bytes 1572888 | tf_op jit(solution)/shard_map/while/body/eval_jaxpr/jit(_take)/gather | solution.py:94
  237.7 4.4 %while.24 = (s32[]{:T(128)}, f32[256,256]{1,0:T(8,128)S(1)}, f32[256]{0:T(256)S(1)}, s32[]{:T(128)}, f32[256,6,128]{2,0,1:T(8,128)S(1)}, /*index=5*/f32[256,6,12...) while((s32[]{:T(128)}, f32[256,256]{1,0:T(8,128)S(1)}, f32[256]{0:T(256)S(1)}, ...), condition=%wide.region_4.5_spmd, body=%wide.region_3.4_spmd.sunk | while | flops 101122304 | bytes 924303 | solution.py:65
  247.1 1.2 fusion.125
  248.3 1.1 copy_dynamic-update-slice_fusion.2
  249.4 38.7 %all_to_all.36 = f32[256,4,4,128]{3,2,1,0:T(4,128)S(1)} all-to-all(f32[256,4,4,128]{3,2,1,0:T(4,128)} %bitcast.153), channel_id=1, replica_groups=mesh['mem'=16,'tile'=32] {'mem'}, dimensions={0} | all-to-all | bytes 4194304 | tf_op jit(solution)/shard_map/all_to_all | solution.py:101
  288.1 1.9 copy.41
  (206 shorter events, 40.0 us)
Async XLA Ops:
  6.5 26.8 %copy-start = (s32[64,6]{0,1:T(8,128)S(1)}, s32[64,6]{0,1:T(8,128)}, u32[]{:S(2)}) copy-start(s32[64,6]{0,1:T(8,128)} %param.17) | copy-start | bytes 4612
  6.5 134.9 %all-gather.2.cloned.1.call-start = ((), (), s32[]{:S(2)}) async-start(), calls=%async_computation.2 | async-start | bytes 13369344 | tf_op jit(solution)/shard_map/all_gather | solution.py:88
  7.6 11.8 %collective-permute-start = (f32[18,16,128]{2,1,0:T(8,128)S(1)}, f32[18,16,128]{2,1,0:T(8,128)S(1)}, u32[]{:S(2)}, u32[]{:S(2)}) collective-permute-start(f32[18,16,128]{2,1,0:T(8,128)S(1)} %get-tuple-element.186), channel_id=1, source_target_pairs={{0,1},{1,2},{2,3},{3,4},{4,5},{5,6},{6,7},{7,8},{8,9},{9,10},{10,1... | collective-permute-start | bytes 442376 | tf_op jit(solution)/shard_map/ppermute | solution.py:16
  7.6 11.8 %collective-permute-start.1 = (f32[18,16,128]{2,1,0:T(8,128)S(1)}, f32[18,16,128]{2,1,0:T(8,128)S(1)}, u32[]{:S(2)}, u32[]{:S(2)}) collective-permute-start(f32[18,16,128]{2,1,0:T(8,128)S(1)} %get-tuple-element.187), channel_id=1, source_target_pairs={{1,0},{2,1},{3,2},{4,3},{5,4},{6,5},{7,6},{8,7},{9,8},{10,9},{11,1... | collective-permute-start | bytes 442376 | tf_op jit(solution)/shard_map/ppermute | solution.py:18
  25.7 7.6 %copy-start.8 = (s32[64]{0:T(128)S(1)}, s32[64]{0:T(128)}, u32[]{:S(2)}) copy-start(s32[64]{0:T(128)} %param.18) | copy-start | bytes 772
  25.7 7.9 %copy-start.7 = (f32[64,6]{0,1:T(8,128)S(1)}, f32[64,6]{0,1:T(8,128)}, u32[]{:S(2)}) copy-start(f32[64,6]{0,1:T(8,128)} %param.19) | copy-start | bytes 4612
  25.7 8.0 %copy-start.4 = (f32[16,64,128]{2,1,0:T(8,128)S(1)}, f32[16,64,128]{2,1,0:T(8,128)}, u32[]{:S(2)}) copy-start(f32[16,64,128]{2,1,0:T(8,128)} %param.14) | copy-start | bytes 1572868
  25.7 8.0 %copy-start.5 = (f32[64,128]{1,0:T(8,128)S(1)}, f32[64,128]{1,0:T(8,128)}, u32[]{:S(2)}) copy-start(f32[64,128]{1,0:T(8,128)} %param.16) | copy-start | bytes 98308
  25.7 8.0 %copy-start.6 = (f32[64,128]{1,0:T(8,128)S(1)}, f32[64,128]{1,0:T(8,128)}, u32[]{:S(2)}) copy-start(f32[64,128]{1,0:T(8,128)} %param.15) | copy-start | bytes 98308
  25.7 39.2 %all-to-all-start = ((f32[16,64,4,128]{3,0,2,1:T(8,128)}), f32[16,64,4,128]{3,0,2,1:T(8,128)S(1)}, u32[]{:S(2)}, u32[]{:S(2)}) async-start(f32[16,64,4,128]{3,0,2,1:T(8,128)} %copy.34), calls=%async_computation | async-start | bytes 4194304 | tf_op jit(solution)/shard_map/all_to_all | solution.py:79
  64.9 1.3 copy-start.3
  157.8 4.2 %copy-start.1 = (f32[256,4,4,128]{3,0,2,1:T(8,128)}, f32[256,4,4,128]{3,0,2,1:T(8,128)S(1)}, u32[]{:S(2)}) copy-start(f32[256,4,4,128]{3,0,2,1:T(8,128)S(1)} %get-tuple-element.399) | copy-start | bytes 6291460 | tf_op jit(solution)/shard_map/while
  180.2 3.4 %copy-start.2 = (f32[256,4,4,128]{3,0,2,1:T(8,128)S(1)}, f32[256,4,4,128]{3,0,2,1:T(8,128)}, u32[]{:S(2)}) copy-start(f32[256,4,4,128]{3,0,2,1:T(8,128)} %copy-done.1) | copy-start | bytes 6291460 | tf_op jit(solution)/shard_map/while
  183.6 4.2 %copy-start.1 = (f32[256,4,4,128]{3,0,2,1:T(8,128)}, f32[256,4,4,128]{3,0,2,1:T(8,128)S(1)}, u32[]{:S(2)}) copy-start(f32[256,4,4,128]{3,0,2,1:T(8,128)S(1)} %get-tuple-element.399) | copy-start | bytes 6291460 | tf_op jit(solution)/shard_map/while
  199.6 3.4 %copy-start.2 = (f32[256,4,4,128]{3,0,2,1:T(8,128)S(1)}, f32[256,4,4,128]{3,0,2,1:T(8,128)}, u32[]{:S(2)}) copy-start(f32[256,4,4,128]{3,0,2,1:T(8,128)} %copy-done.1) | copy-start | bytes 6291460 | tf_op jit(solution)/shard_map/while
  203.0 4.2 %copy-start.1 = (f32[256,4,4,128]{3,0,2,1:T(8,128)}, f32[256,4,4,128]{3,0,2,1:T(8,128)S(1)}, u32[]{:S(2)}) copy-start(f32[256,4,4,128]{3,0,2,1:T(8,128)S(1)} %get-tuple-element.399) | copy-start | bytes 6291460 | tf_op jit(solution)/shard_map/while
  224.1 3.4 %copy-start.2 = (f32[256,4,4,128]{3,0,2,1:T(8,128)S(1)}, f32[256,4,4,128]{3,0,2,1:T(8,128)}, u32[]{:S(2)}) copy-start(f32[256,4,4,128]{3,0,2,1:T(8,128)} %copy-done.1) | copy-start | bytes 6291460 | tf_op jit(solution)/shard_map/while
  227.5 4.2 %copy-start.1 = (f32[256,4,4,128]{3,0,2,1:T(8,128)}, f32[256,4,4,128]{3,0,2,1:T(8,128)S(1)}, u32[]{:S(2)}) copy-start(f32[256,4,4,128]{3,0,2,1:T(8,128)S(1)} %get-tuple-element.399) | copy-start | bytes 6291460 | tf_op jit(solution)/shard_map/while
  246.1 3.4 %copy-start.2 = (f32[256,4,4,128]{3,0,2,1:T(8,128)S(1)}, f32[256,4,4,128]{3,0,2,1:T(8,128)}, u32[]{:S(2)}) copy-start(f32[256,4,4,128]{3,0,2,1:T(8,128)} %copy-done.1) | copy-start | bytes 6291460 | tf_op jit(solution)/shard_map/while
Sparse Core Ops, SparseCore 0:
  21.7 119.7 all-gather.1
where the time goes:
time: 302 us; the launch traced here: 297 us
  waiting for transfers between devices  107 us (35%)
  local copies, waits for them, and re-layouts  62.5 us (21%)
  blocking collectives  38.7 us (13%)
  matrix products  28.6 us (9%)
  loops' own time  21.5 us (7%)
  starting transfers between devices  16.5 us (5%)
  between operations  13.5 us (4%)
  other arithmetic  8.23 us (3%)
    all_gather x1, waiting for transfers between devices, per_device(): prior_all = lax.all_gather(prior_rim, 'mem', axis=0, tiled=True)  73.4 us
    all_to_all x1, blocking collectives, per_device(): lax.all_to_all(updated, 'mem', split_axis=0, concat_axis=1, tiled=True)  38.7 us
    all_to_all x1, waiting for transfers between devices, per_device(): lax.all_to_all(state, 'mem', split_axis=1, concat_axis=0, tiled=True)  31.1 us
    gather x4, local copies, waits for them, and re-layouts, run_tile(): prior = jnp.take(prior_all, positions[number], axis=1)  20.7 us
    while x1, local copies, waits for them, and re-layouts, per_device(): updated = lax.map(run_tile, jnp.arange(tiles_here, dtype=jnp.int32))  16.4 us
    another operation x4, loops' own time, update_tile(): gram, proj = lax.fori_loop(0, count, add_slot, start)  11.2 us
    another operation x1, loops' own time, per_device(): updated = lax.map(run_tile, jnp.arange(tiles_here, dtype=jnp.int32))  10.3 us
    ppermute x1, starting transfers between devices, extended(): lax.ppermute(head, axis, [((i + 1) % count, i) for i in range(count)])  8.95 us
  transfers between devices with their start and end apart: 4, of which 3 were waited for; matrix products, arithmetic and copies ran while one was open for 2% of the time, Pallas kernels for 0%

commit v1 on v0

v1 whole, which is shorter than its diff:
```python
import jax
import jax.numpy as jnp
from jax import lax
from jax.experimental import pallas as pl
from jax.experimental.pallas import tpu as pltpu
from jax.sharding import PartitionSpec as P

MESH = pl.DeviceIdType.MESH
MEMBERS = 256
SLOTS = 6
PER = 4
WINDOW = 36

F32 = jnp.float32
BF16 = jnp.bfloat16
NN = (((1,), (0,)), ((), ()))
NT = (((1,), (1,)), ((), ()))


def split(x):
    high = x.astype(BF16)
    return high, (x - high.astype(F32)).astype(BF16)


def mxu(a, b, dims=NN):
    return lax.dot_general(a, b, dims, preferred_element_type=F32)


def mul(a, b, dims=NN):
    ah, al = a
    bh, bl = b
    return mxu(ah, bh, dims) + (mxu(ah, bl, dims) + mxu(al, bh, dims))


def transform(gram, proj):
    rows = lax.broadcasted_iota(jnp.int32, (MEMBERS, MEMBERS), 0)
    cols = lax.broadcasted_iota(jnp.int32, (MEMBERS, MEMBERS), 1)
    diag = rows == cols
    ident = diag.astype(F32)
    amat = (MEMBERS - 1.0) * ident + gram
    scale = jnp.sqrt(jnp.sum(amat * amat, keepdims=True))
    root = amat * (1.0 / scale)
    first = 1.5 * ident - 0.5 * root
    root_s = split(root)
    first_s = split(first)
    square = mul(root_s, root_s)
    inner = mul(first_s, split(1.5 * root - 0.5 * square))
    second = 1.5 * ident - 0.5 * inner
    second_s = split(second)
    r = mul(second_s, second_s)
    poly = 1.5 * second + mul(split(r), split(r - 1.5 * second))
    inverse = mul(first_s, split(poly))
    once = jnp.sum(inverse * proj, axis=0, keepdims=True)
    twice = jnp.sum(inverse * once, axis=1, keepdims=True) * (1.0 / scale)
    wmean = jnp.sum(jnp.where(diag, twice, 0.0), axis=0, keepdims=True)
    full = jnp.sqrt((MEMBERS - 1.0) / scale) * inverse + wmean
    return full - jnp.mean(full, axis=1, keepdims=True) + 1.0 / MEMBERS


def kernel(
    st_hbm, ob_hbm, val_hbm, prec_hbm, itab_hbm, ftab_hbm,
    out_ref,
    st_in, st_t, ob_in, ob_t, obs, xbuf, obuf, vals, precs, itab, ftab, itab_s, ftab_s,
    vh, vl, local_sem, tab_send, tab_recv, aux_send, aux_recv, ob_send, ob_recv, pair_send, st_send, st_recv, out_send, out_recv,
):
    m = lax.axis_index("mem")
    i = lax.axis_index("tile")
    q = lax.rem(i, 2)
    z = i // 2
    g = 16 * z + m
    sib = (m, i + 1 - 2 * q)
    src_shard = g // 8
    home = src_shard == i

    load_ob = pltpu.make_async_copy(ob_hbm, ob_in, local_sem.at[0])
    load_st = pltpu.make_async_copy(st_hbm, st_in, local_sem.at[1])
    load_ob.start()
    load_st.start()

    barrier = pltpu.get_barrier_semaphore()

    def greet(device):
        pl.semaphore_signal(barrier, inc=1, device_id=device, device_id_type=MESH)

    def greet_source(j, c):
        @pl.when(jnp.logical_not(home & (j == m)))
        def _():
            greet((j, src_shard))
        return c

    def greet_owner(j, c):
        md, td = 8 * q + j // 2, 2 * z + lax.rem(j, 2)

        @pl.when(jnp.logical_not((md == m) & (td == i)))
        def _():
            greet((md, td))
        return c

    def greet_edge(j, c):
        greet((j, lax.rem(src_shard + 2 * q - 1 + 32, 32)))
        return c

    lax.fori_loop(0, 16, greet_source, 0)
    lax.fori_loop(0, 16, greet_owner, 0)
    edge = ((q == 0) & (lax.rem(g, 8) <= 1)) | ((q == 1) & (lax.rem(g, 8) >= 6))

    @pl.when(edge)
    def _():
        lax.fori_loop(0, 16, greet_edge, 0)

    greet(sib)
    greet((m, lax.rem(2 * z + 31, 32)))
    greet((m, lax.rem(2 * z + 2, 32)))

    load_ob.wait()

    def turn_ob(b, c):
        for k in range(4):
            ob_t[4 * b + k] = ob_in[pl.ds(4 * b + k, 16, stride=64), :]
        return c

    lax.fori_loop(0, 16, turn_ob, 0)

    @pl.when(home)
    def _():
        pl.semaphore_wait(barrier, 37)

    @pl.when(jnp.logical_not(home))
    def _():
        pl.semaphore_wait(barrier, 39)

    def remote(src, dst, ss, rs, device):
        return pltpu.make_async_remote_copy(src_ref=src, dst_ref=dst, send_sem=ss, recv_sem=rs, device_id=device, device_id_type=MESH)

    own_itab = pltpu.make_async_copy(itab_hbm, itab.at[0], local_sem.at[2])
    own_ftab = pltpu.make_async_copy(ftab_hbm, ftab.at[0], local_sem.at[3])
    own_itab.start()
    own_ftab.start()
    tabs = [
        remote(itab_hbm, itab.at[1], tab_send.at[0], tab_recv.at[0], sib),
        remote(ftab_hbm, ftab.at[1], tab_send.at[1], tab_recv.at[1], sib),
    ]
    far = 2 * lax.rem(z + 2 * q - 1 + 16, 16)
    auxes = []
    owns = []
    for n, (hbm, buf) in enumerate(((val_hbm, vals), (prec_hbm, precs))):
        owns.append(pltpu.make_async_copy(hbm, buf.at[q + 1], aux_recv.at[n, q + 1]))
        auxes.append(remote(hbm, buf.at[q + 1], aux_send.at[n, 0], aux_recv.at[n, q + 1], sib))
        for core in range(2):
            auxes.append(remote(hbm, buf.at[3 - 3 * q], aux_send.at[n, 1 + core], aux_recv.at[n, 3 - 3 * q], (m, far + core)))
    for copy in tabs + owns + auxes:
        copy.start()

    def ob_unit(w, k):
        kk = lax.rem(k + m, 8)
        gd = lax.rem(8 * i + kk + 2 - w // 2 + 256, 256)
        md, td = lax.rem(gd, 16), 2 * (gd // 16) + w // 5
        src = ob_t.at[pl.ds(4 * (2 * kk + w % 2), 4)]
        dst = obs.at[pl.ds(4 * (w - w // 5), 4), pl.ds(pl.multiple_of(16 * m, 16), 16)]
        away = remote(src, dst, ob_send.at[w, k], ob_recv.at[w], (md, td))
        stay = pltpu.make_async_copy(src, dst, ob_recv.at[w])
        return (md == m) & (td == i), away, stay

    order = (1, 5, 2, 6, 3, 7, 4, 8, 0, 9)
    for w in order:
        def send_ob(k, c):
            here, away, stay = ob_unit(w, k)

            @pl.when(here)
            def _():
                stay.start()

            @pl.when(jnp.logical_not(here))
            def _():
                away.start()
            return c

        lax.fori_loop(0, 8, send_ob, 0)

    load_st.wait()

    def turn_st(b, c):
        for k in range(8):
            st_t[8 * b + k] = st_in[pl.ds(8 * b + k, 16, stride=256), :]
        return c

    lax.fori_loop(0, 32, turn_st, 0)

    def st_unit(t, j):
        kk, core = lax.rem(j // 2 + m, 8), lax.rem(j, 2)
        md, td = 8 * q + kk, 2 * z + core
        src = st_t.at[pl.ds(16 * (2 * kk + core) + 4 * t, 4)]
        dst = xbuf.at[pl.ds(4 * t, 4), pl.ds(pl.multiple_of(16 * m, 16), 16)]
        away = remote(src, dst, st_send.at[t, j], st_recv.at[t], (md, td))
        stay = pltpu.make_async_copy(src, dst, st_recv.at[t])
        return (md == m) & (td == i), away, stay

    for t in range(PER):
        def send_st(j, c):
            here, away, stay = st_unit(t, j)

            @pl.when(here)
            def _():
                stay.start()

            @pl.when(jnp.logical_not(here))
            def _():
                away.start()
            return c

        lax.fori_loop(0, 16, send_st, 0)

    own_itab.wait()
    own_ftab.wait()
    for copy in tabs:
        copy.wait_recv()
    which = jnp.where(home, 0, 1)
    to_smem = [
        pltpu.make_async_copy(itab.at[which], itab_s, local_sem.at[4]),
        pltpu.make_async_copy(ftab.at[which], ftab_s, local_sem.at[5]),
    ]
    for copy in to_smem:
        copy.start()
    for copy in to_smem:
        copy.wait()
    for n, (hbm, buf) in enumerate(((val_hbm, vals), (prec_hbm, precs))):
        for slot in range(4):
            pltpu.make_async_copy(hbm, buf.at[slot], aux_recv.at[n, slot]).wait()

    def ob_block(w, slot):
        ref = obs.at[pl.ds(4 * slot, 4)]
        return pltpu.make_async_copy(ref, ref, ob_recv.at[w])

    pairs = []
    for e in range(4):
        w = 1 + 4 * q + e
        ob_block(w, w - q).wait()
        copy = remote(obs.at[pl.ds(4 * (w - q), 4)], obs.at[pl.ds(4 * (w - 1 + q), 4)], pair_send.at[e], ob_recv.at[w], sib)
        copy.start()
        pairs.append(copy)
    ob_block(9 * q, 8 * q).wait()
    for e in range(4):
        w = 5 - 4 * q + e
        ob_block(w, w - q).wait()

    def tile_step(t, c):
        row = 8 * lax.rem(g, 8) + 4 * q + t
        line, base = row // 8, 16 * lax.rem(row, 8)
        count = itab_s[line, base + SLOTS]
        proj = jnp.zeros((MEMBERS, 128), F32)
        for s in range(SLOTS):
            batch = itab_s[line, base + s]
            place = lax.rem(batch - (8 * g - 16 + 4 * q) + 4096, 2048)
            place = jnp.clip(place, 0, WINDOW - 1)
            where = lax.rem(batch - (128 * z - 64) + 4096, 2048)
            where = jnp.clip(where, 0, 255)
            shard, line_b = where // 64, lax.rem(where, 64)
            prior = obs[place]
            value = vals[shard, pl.ds(line_b, 1), :]
            prec = precs[shard, pl.ds(line_b, 1), :]
            weight = jnp.where(s < count, ftab_s[line, base + s], 0.0)
            size = jnp.sqrt(prec * weight)
            ymean = jnp.mean(prior, axis=0, keepdims=True)
            scaled = (prior - ymean) * size
            proj = proj + scaled * ((value - ymean) * size)
            high, low = split(scaled)
            vh[:, 128 * s : 128 * (s + 1)] = high
            vl[:, 128 * s : 128 * (s + 1)] = low
        both = (vh[...], vl[...])
        gram = mul(both, both, NT)
        turn = transform(gram, jnp.sum(proj, axis=1, keepdims=True))
        turn_s = split(turn)

        whole = xbuf.at[pl.ds(4 * t, 4)]
        pltpu.make_async_copy(whole, whole, st_recv.at[t]).wait()
        for half in range(2):
            x = jnp.concatenate([xbuf[4 * t + 2 * half], xbuf[4 * t + 2 * half + 1]], axis=1)
            moved = mul(turn_s, split(x))
            obuf[4 * t + 2 * half] = moved[:, :128]
            obuf[4 * t + 2 * half + 1] = moved[:, 128:]

        def send_out(j, c):
            md = lax.rem(j + m, 16)
            here, away, stay = out_unit(t, j)

            @pl.when(here)
            def _():
                stay.start()

            @pl.when(jnp.logical_not(here))
            def _():
                away.start()
            return c

        lax.fori_loop(0, 16, send_out, 0)
        return c

    def out_unit(t, j):
        md = lax.rem(j + m, 16)
        row = 4 * (8 * lax.rem(g, 8) + 4 * q + t)
        src = obuf.at[pl.ds(4 * t, 4), pl.ds(pl.multiple_of(16 * md, 16), 16)]
        dst = out_ref.at[pl.ds(row, 4)]
        away = remote(src, dst, out_send.at[t, j], out_recv.at[0], (md, src_shard))
        stay = pltpu.make_async_copy(src, dst, out_recv.at[0])
        return (md == m) & home, away, stay

    lax.fori_loop(0, PER, tile_step, 0)

    for copy in tabs + auxes:
        copy.wait_send()
    for copy in pairs:
        copy.wait_send()
    for w in range(10):
        def left_ob(k, c):
            here, away, stay = ob_unit(w, k)

            @pl.when(jnp.logical_not(here))
            def _():
                away.wait_send()
            return c

        lax.fori_loop(0, 8, left_ob, 0)

    def left_t(t, c):
        def left_j(j, c):
            here, away, stay = st_unit(t, j)

            @pl.when(jnp.logical_not(here))
            def _():
                away.wait_send()
            here, away, stay = out_unit(t, j)

            @pl.when(jnp.logical_not(here))
            def _():
                away.wait_send()
            return c

        return lax.fori_loop(0, 16, left_j, c)

    lax.fori_loop(0, PER, left_t, 0)
    pltpu.make_async_copy(out_ref, out_ref, out_recv.at[0]).wait()


def per_device(state, obs_prior, obs_value, obs_prec, tile_batches, tile_count, loc_weight):
    itab = jnp.concatenate([tile_batches, tile_count[:, None], jnp.zeros((64, 9), jnp.int32)], axis=1).reshape(8, 128)
    ftab = jnp.concatenate([loc_weight, jnp.zeros((64, 10), F32)], axis=1).reshape(8, 128)
    anywhere = pl.BlockSpec(memory_space=pl.ANY)
    dma = pltpu.SemaphoreType.DMA
    out = pl.pallas_call(
        kernel,
        out_shape=jax.ShapeDtypeStruct((256, 16, 128), F32),
        in_specs=[anywhere] * 6,
        out_specs=anywhere,
        scratch_shapes=[
            pltpu.VMEM((16 * 256, 128), F32),
            pltpu.VMEM((256, 16, 128), F32),
            pltpu.VMEM((16 * 64, 128), F32),
            pltpu.VMEM((64, 16, 128), F32),
            pltpu.VMEM((WINDOW, MEMBERS, 128), F32),
            pltpu.VMEM((16, MEMBERS, 128), F32),
            pltpu.VMEM((16, MEMBERS, 128), F32),
            pltpu.VMEM((4, 64, 128), F32),
            pltpu.VMEM((4, 64, 128), F32),
            pltpu.VMEM((2, 8, 128), jnp.int32),
            pltpu.VMEM((2, 8, 128), F32),
            pltpu.SMEM((8, 128), jnp.int32),
            pltpu.SMEM((8, 128), F32),
            pltpu.VMEM((MEMBERS, SLOTS * 128), BF16),
            pltpu.VMEM((MEMBERS, SLOTS * 128), BF16),
            dma((6,)),
            dma((2,)),
            dma((2,)),
            dma((2, 3)),
            dma((2, 4)),
            dma((10, 8)),
            dma((10,)),
            dma((4,)),
            dma((4, 16)),
            dma((4,)),
            dma((4, 16)),
            dma((1,)),
        ],
        compiler_params=pltpu.CompilerParams(collective_id=0, has_side_effects=True, vmem_limit_bytes=48 * 2**20),
        name="etkf",
    )(
        state.reshape(16 * 256, 128),
        obs_prior.reshape(16 * 64, 128),
        obs_value,
        obs_prec,
        itab,
        ftab,
    )
    return jnp.transpose(out, (1, 0, 2)).reshape(16, 64, 4, 128)


def solution(mesh):
    in_specs = (
        P("mem", "tile", None, None),
        P("mem", "tile", None),
        P("tile", None),
        P("tile", None),
        P("tile", None),
        P("tile"),
        P("tile", None),
    )
    out_specs = P("mem", "tile", None, None)
    return jax.shard_map(
        per_device, mesh=mesh, in_specs=in_specs, out_specs=out_specs, check_vma=False
    )
```

time: 302 us -> 113 us (0.37)
  the two profiles are of different devices: /device:TPU:6 before, /device:TPU:2 now
where the time goes in v1:
time: 113 us; the launch traced here: 112 us
  Pallas kernels  104 us (92%)
  local copies, waits for them, and re-layouts  7.38 us (7%)
    pallas_call x1, Pallas kernels, per_device(): pl.pallas_call(kernel, out_shape=jax.ShapeDtypeStruct((256, 16, 128), F32...  104 us
    unnamed x9, local copies, waits for them, and re-layouts  4.93 us

profile of v1, /device:TPU:2, one launch (start us, length us, event | category | flops | bytes accessed | tf_op | source)
XLA Modules:
  0.0 112.3 jit_solution(15432419105613106546)
XLA Ops:
  0.0 0.1 pad.3.clone
  0.1 0.8 add_add_fusion
  0.9 0.1 copy.16
  0.9 0.1 reshape.17.itab_hbm
  1.0 0.8 copy.19
  1.8 0.1 reshape.18.ftab_hbm
  1.9 0.0 copy-start
  1.9 1.6 %copy-done = f32[16,64,4,128]{3,2,1,0:T(4,128)S(1)} copy-done((f32[16,64,4,128]{3,2,1,0:T(4,128)S(1)}, f32[16,64,4,128]{3,2,1,0:T(4,128)}, u32[]{:S(2)}) %copy-start) | copy-done | bytes 2097176
  3.5 0.0 copy-start.1
  3.5 1.0 copy-done.1
  4.5 0.0 copy-start.2
  4.5 0.8 copy-done.2
  5.3 0.0 copy-start.3
  5.3 0.8 copy-done.3
  6.0 104.2 %etkf.1 = f32[256,16,128]{2,1,0:T(8,128)S(1)} custom-call(f32[4096,128]{1,0:T(8,128)S(1)} %bitcast.7, f32[1024,128]{1,0:T(8,128)S(1)} %bitcast.8, f32[64,128]{1,0:T(8,128)S(1)} %copy-done.2, f32[64,128]{1,0:T(8,128)S(1)} %copy-done.3, s32[8,128]{1,0:T(8,128)S(1)} %reshape.17.itab_hbm, f32[8,128]{1,0:T(8,128)S(1)} %reshape.18.ftab_hbm), custom_call_target="tpu_custom_call" | custom-call | tf_op jit(solution)/shard_map/etkf/pallas_call | solution.py:349
  110.2 2.1 %copy.18 = f32[16,64,4,128]{3,2,1,0:T(4,128)} copy(f32[16,64,4,128]{3,0,2,1:T(8,128)S(1)} %bitcast.6) | data formatting | bytes 4194304 | tf_op jit(solution)/shard_map/reshape | solution.py:393
  (2 shorter events, 0.0 us)
Async XLA Ops:
  1.9 1.6 %copy-start = (f32[16,64,4,128]{3,2,1,0:T(4,128)S(1)}, f32[16,64,4,128]{3,2,1,0:T(4,128)}, u32[]{:S(2)}) copy-start(f32[16,64,4,128]{3,2,1,0:T(4,128)} %param.7) | copy-start | bytes 6291460
  3.5 1.0 copy-start.1
  4.5 0.8 copy-start.2
  5.3 0.8 copy-start.3

commit v2 on v1

v2 whole, which is shorter than its diff:
```python
import jax
import jax.numpy as jnp
from jax import lax
from jax.experimental import pallas as pl
from jax.experimental.pallas import tpu as pltpu
from jax.sharding import PartitionSpec as P

MESH = pl.DeviceIdType.MESH
MEMBERS = 256
SLOTS = 6
PER = 4
WINDOW = 36
STEP = 1
OSTEP = 1
GROUPS = ((0, 2), (2, 2), (4, 1), (5, 1), (6, 2), (8, 2))
ORDER = (2, 3, 1, 4, 0, 5)

F32 = jnp.float32
BF16 = jnp.bfloat16
NN = (((1,), (0,)), ((), ()))
NT = (((1,), (1,)), ((), ()))


def split(x):
    high = x.astype(BF16)
    return high, (x - high.astype(F32)).astype(BF16)


def mxu(a, b, dims=NN):
    return lax.dot_general(a, b, dims, preferred_element_type=F32)


def mul(a, b, dims=NN):
    ah, al = a
    bh, bl = b
    return mxu(ah, bh, dims) + (mxu(ah, bl, dims) + mxu(al, bh, dims))


def transform(gram, proj):
    rows = lax.broadcasted_iota(jnp.int32, (MEMBERS, MEMBERS), 0)
    cols = lax.broadcasted_iota(jnp.int32, (MEMBERS, MEMBERS), 1)
    diag = rows == cols
    ident = diag.astype(F32)
    amat = (MEMBERS - 1.0) * ident + gram
    scale = jnp.sqrt(jnp.sum(amat * amat, keepdims=True))
    root = amat * (1.0 / scale)
    first = 1.5 * ident - 0.5 * root
    root_s = split(root)
    first_s = split(first)
    square = mul(root_s, root_s)
    inner = mul(first_s, split(1.5 * root - 0.5 * square))
    second = 1.5 * ident - 0.5 * inner
    second_s = split(second)
    r = mul(second_s, second_s)
    poly = 1.5 * second + mul(split(r), split(r - 1.5 * second))
    inverse = mul(first_s, split(poly))
    once = jnp.sum(inverse * proj, axis=0, keepdims=True)
    twice = jnp.sum(inverse * once, axis=1, keepdims=True) * (1.0 / scale)
    wmean = jnp.sum(jnp.where(diag, twice, 0.0), axis=0, keepdims=True)
    full = jnp.sqrt((MEMBERS - 1.0) / scale) * inverse + wmean
    return full - jnp.mean(full, axis=1, keepdims=True) + 1.0 / MEMBERS


def kernel(
    st_hbm, ob_hbm, val_hbm, prec_hbm, itab_hbm, ctab_hbm, ftab_hbm,
    out_ref,
    st_in, st_t, ob_in, ob_t, obs, xbuf, obuf, vals, precs, itab, ctab, ftab, itab_s, ctab_s, ftab_s,
    vh, vl, th, tl, local_sem, tab_send, tab_recv, aux_send, aux_recv, ob_send, ob_recv, pair_send, pair_recv, st_send, st_recv, out_send, out_recv,
):
    m = lax.axis_index("mem")
    i = lax.axis_index("tile")
    q = lax.rem(i, 2)
    z = i // 2
    g = 16 * z + m
    sib = (m, i + 1 - 2 * q)
    src_shard = g // 8
    home = src_shard == i

    load_ob = pltpu.make_async_copy(ob_hbm, ob_in, local_sem.at[0])
    load_st = pltpu.make_async_copy(st_hbm, st_in, local_sem.at[1])
    load_ob.start()
    load_st.start()

    barrier = pltpu.get_barrier_semaphore()

    def greet(device):
        pl.semaphore_signal(barrier, inc=1, device_id=device, device_id_type=MESH)

    def greet_source(j, c):
        @pl.when(jnp.logical_not(home & (j == m)))
        def _():
            greet((j, src_shard))
        return c

    def greet_owner(j, c):
        md, td = 8 * q + j // 2, 2 * z + lax.rem(j, 2)

        @pl.when(jnp.logical_not((md == m) & (td == i)))
        def _():
            greet((md, td))
        return c

    def greet_edge(j, c):
        greet((j, lax.rem(src_shard + 2 * q - 1 + 32, 32)))
        return c

    lax.fori_loop(0, 16, greet_source, 0)
    lax.fori_loop(0, 16, greet_owner, 0)
    edge = ((q == 0) & (lax.rem(g, 8) <= 1)) | ((q == 1) & (lax.rem(g, 8) >= 6))

    @pl.when(edge)
    def _():
        lax.fori_loop(0, 16, greet_edge, 0)

    greet(sib)
    greet((m, lax.rem(2 * z + 31, 32)))
    greet((m, lax.rem(2 * z + 2, 32)))

    load_ob.wait()

    def turn_ob(b, c):
        for k in range(4):
            ob_t[4 * b + k] = ob_in[pl.ds(4 * b + k, 16, stride=64), :]
        return c

    lax.fori_loop(0, 16, turn_ob, 0)

    @pl.when(home)
    def _():
        pl.semaphore_wait(barrier, 37)

    @pl.when(jnp.logical_not(home))
    def _():
        pl.semaphore_wait(barrier, 39)

    def remote(src, dst, ss, rs, device):
        return pltpu.make_async_remote_copy(src_ref=src, dst_ref=dst, send_sem=ss, recv_sem=rs, device_id=device, device_id_type=MESH)

    tables = ((itab_hbm, itab, itab_s), (ctab_hbm, ctab, ctab_s), (ftab_hbm, ftab, ftab_s))
    own_tabs, tabs = [], []
    for n, (hbm, buf, smem) in enumerate(tables):
        own_tabs.append(pltpu.make_async_copy(hbm, buf.at[0], local_sem.at[2 + n]))
        tabs.append(remote(hbm, buf.at[1], tab_send.at[n], tab_recv.at[n], sib))
    far = 2 * lax.rem(z + 2 * q - 1 + 16, 16)
    auxes = []
    owns = []
    for n, (hbm, buf) in enumerate(((val_hbm, vals), (prec_hbm, precs))):
        owns.append(pltpu.make_async_copy(hbm, buf.at[q + 1], aux_recv.at[n, q + 1]))
        auxes.append(remote(hbm, buf.at[q + 1], aux_send.at[n, 0], aux_recv.at[n, q + 1], sib))
        for core in range(2):
            auxes.append(remote(hbm, buf.at[3 - 3 * q], aux_send.at[n, 1 + core], aux_recv.at[n, 3 - 3 * q], (m, far + core)))
    for copy in own_tabs + tabs + owns + auxes:
        copy.start()

    def ob_group(n, k):
        w, size = GROUPS[n]
        core = w // 5
        kk = lax.rem(k + m, 8)
        gd = lax.rem(8 * i + kk + 2 - w // 2 + 256, 256)
        md, td = lax.rem(gd, 16), 2 * (gd // 16) + core
        src = ob_t.at[pl.ds(4 * (2 * kk + w % 2), 4 * size)]
        dst = obs.at[pl.ds(4 * (w - core), 4 * size), pl.ds(pl.multiple_of(16 * m, 16), 16)]

        def away():
            return remote(src, dst, ob_send.at[n, k], ob_recv.at[n], (md, td))

        def stay():
            return pltpu.make_async_copy(src, dst, ob_recv.at[n])

        return (md == m) & (td == i), away, stay

    def launch(unit):
        here, away, stay = unit

        @pl.when(here)
        def _():
            stay().start()

        @pl.when(jnp.logical_not(here))
        def _():
            away().start()

    def left(unit):
        here, away, stay = unit

        @pl.when(jnp.logical_not(here))
        def _():
            away().wait_send()

    def each(count, act):
        def body(j, c):
            act(j)
            return c

        lax.fori_loop(0, count, body, 0)

    for n in ORDER:
        each(8, lambda k: launch(ob_group(n, k)))

    load_st.wait()

    def turn_st(b, c):
        for k in range(8):
            st_t[8 * b + k] = st_in[pl.ds(8 * b + k, 16, stride=256), :]
        return c

    lax.fori_loop(0, 32, turn_st, 0)

    def st_unit(t, j):
        kk, core = lax.rem(j // 2 + m, 8), lax.rem(j, 2)
        md, td = 8 * q + kk, 2 * z + core
        src = st_t.at[pl.ds(16 * (2 * kk + core) + 4 * STEP * t, 4 * STEP)]
        dst = xbuf.at[pl.ds(4 * STEP * t, 4 * STEP), pl.ds(pl.multiple_of(16 * m, 16), 16)]

        def away():
            return remote(src, dst, st_send.at[t, j], st_recv.at[t], (md, td))

        def stay():
            return pltpu.make_async_copy(src, dst, st_recv.at[t])

        return (md == m) & (td == i), away, stay

    for t in range(PER // STEP):
        each(16, lambda j: launch(st_unit(t, j)))

    for copy in own_tabs:
        copy.wait()
    for copy in tabs:
        copy.wait_recv()
    which = jnp.where(home, 0, 1)
    to_smem = []
    for n, (hbm, buf, smem) in enumerate(tables):
        to_smem.append(pltpu.make_async_copy(buf.at[which], smem, local_sem.at[5 + n]))
    for copy in to_smem:
        copy.start()
    for copy in to_smem:
        copy.wait()
    for n, (hbm, buf) in enumerate(((val_hbm, vals), (prec_hbm, precs))):
        for slot in range(4):
            pltpu.make_async_copy(hbm, buf.at[slot], aux_recv.at[n, slot]).wait()

    def landed(slot, size, sem):
        ref = obs.at[pl.ds(slot, size)]
        pltpu.make_async_copy(ref, ref, sem).wait()

    landed(16 * q, 8, ob_recv.at[5 * q])
    landed(8 + 16 * q, 8, ob_recv.at[1 + 3 * q])
    landed(16, 4, ob_recv.at[2 + q])
    pair = remote(obs.at[pl.ds(4 + 12 * q, 16)], obs.at[pl.ds(20 * q, 16)], pair_send.at[0], pair_recv.at[0], sib)
    pair.start()
    landed(20 - 20 * q, 16, pair_recv.at[0])

    def tile_step(t, c):
        row = 8 * lax.rem(g, 8) + 4 * q + t
        count = ctab_s[0, row]
        proj = jnp.zeros((MEMBERS, 128), F32)
        for s in range(SLOTS):
            batch = itab_s[s, row]
            place = lax.rem(batch - (8 * g - 16 + 4 * q) + 4096, 2048)
            place = jnp.clip(place, 0, WINDOW - 1)
            where = lax.rem(batch - (128 * z - 64) + 4096, 2048)
            where = jnp.clip(where, 0, 255)
            shard, line_b = where // 64, lax.rem(where, 64)
            prior = obs[place]
            value = vals[shard, pl.ds(line_b, 1), :]
            prec = precs[shard, pl.ds(line_b, 1), :]
            weight = jnp.where(s < count, ftab_s[s, row], 0.0)
            size = jnp.sqrt(prec * weight)
            ymean = jnp.mean(prior, axis=0, keepdims=True)
            scaled = (prior - ymean) * size
            proj = proj + scaled * ((value - ymean) * size)
            high, low = split(scaled)
            vh[:, 128 * s : 128 * (s + 1)] = high
            vl[:, 128 * s : 128 * (s + 1)] = low
        both = (vh[...], vl[...])
        gram = mul(both, both, NT)
        turn = transform(gram, jnp.sum(proj, axis=1, keepdims=True))
        high, low = split(turn)
        th[t] = high
        tl[t] = low
        return c

    def apply_step(t, c):
        turn_s = (th[t], tl[t])

        @pl.when(lax.rem(t, STEP) == 0)
        def _():
            whole = xbuf.at[pl.ds(4 * t, 4 * STEP)]
            pltpu.make_async_copy(whole, whole, st_recv.at[t // STEP]).wait()

        for half in range(2):
            x = jnp.concatenate([xbuf[4 * t + 2 * half], xbuf[4 * t + 2 * half + 1]], axis=1)
            moved = mul(turn_s, split(x))
            obuf[4 * t + 2 * half] = moved[:, :128]
            obuf[4 * t + 2 * half + 1] = moved[:, 128:]

        @pl.when(lax.rem(t, OSTEP) == OSTEP - 1)
        def _():
            each(16, lambda j: launch(out_unit(t // OSTEP, j)))

        return c

    def out_unit(t, j):
        md = lax.rem(j + m, 16)
        row = 4 * (8 * lax.rem(g, 8) + 4 * q + OSTEP * t)
        src = obuf.at[pl.ds(4 * OSTEP * t, 4 * OSTEP), pl.ds(pl.multiple_of(16 * md, 16), 16)]
        dst = out_ref.at[pl.ds(row, 4 * OSTEP)]

        def away():
            return remote(src, dst, out_send.at[t, j], out_recv.at[0], (md, src_shard))

        def stay():
            return pltpu.make_async_copy(src, dst, out_recv.at[0])

        return (md == m) & home, away, stay

    lax.fori_loop(0, PER, tile_step, 0)
    lax.fori_loop(0, PER, apply_step, 0)

    for copy in tabs + auxes:
        copy.wait_send()
    pair.wait_send()
    for n in range(len(GROUPS)):
        each(8, lambda k: left(ob_group(n, k)))
    for t in range(PER // STEP):
        each(16, lambda j: left(st_unit(t, j)))
    for t in range(PER // OSTEP):
        each(16, lambda j: left(out_unit(t, j)))
    pltpu.make_async_copy(out_ref, out_ref, out_recv.at[0]).wait()


def per_device(state, obs_prior, obs_value, obs_prec, tile_batches, tile_count, loc_weight):
    anywhere = pl.BlockSpec(memory_space=pl.ANY)
    dma = pltpu.SemaphoreType.DMA
    out = pl.pallas_call(
        kernel,
        out_shape=jax.ShapeDtypeStruct((256, 16, 128), F32),
        in_specs=[anywhere] * 7,
        out_specs=anywhere,
        scratch_shapes=[
            pltpu.VMEM((16 * 256, 128), F32),
            pltpu.VMEM((256, 16, 128), F32),
            pltpu.VMEM((16 * 64, 128), F32),
            pltpu.VMEM((64, 16, 128), F32),
            pltpu.VMEM((WINDOW, MEMBERS, 128), F32),
            pltpu.VMEM((16, MEMBERS, 128), F32),
            pltpu.VMEM((16, MEMBERS, 128), F32),
            pltpu.VMEM((4, 64, 128), F32),
            pltpu.VMEM((4, 64, 128), F32),
            pltpu.VMEM((2, SLOTS, 64), jnp.int32),
            pltpu.VMEM((2, 1, 64), jnp.int32),
            pltpu.VMEM((2, SLOTS, 64), F32),
            pltpu.SMEM((SLOTS, 64), jnp.int32),
            pltpu.SMEM((1, 64), jnp.int32),
            pltpu.SMEM((SLOTS, 64), F32),
            pltpu.VMEM((MEMBERS, SLOTS * 128), BF16),
            pltpu.VMEM((MEMBERS, SLOTS * 128), BF16),
            pltpu.VMEM((PER, MEMBERS, MEMBERS), BF16),
            pltpu.VMEM((PER, MEMBERS, MEMBERS), BF16),
            dma((8,)),
            dma((3,)),
            dma((3,)),
            dma((2, 3)),
            dma((2, 4)),
            dma((6, 8)),
            dma((6,)),
            dma((1,)),
            dma((1,)),
            dma((4, 16)),
            dma((4,)),
            dma((4, 16)),
            dma((1,)),
        ],
        compiler_params=pltpu.CompilerParams(collective_id=0, has_side_effects=True, vmem_limit_bytes=60 * 2**20),
        name="etkf",
    )(
        state.reshape(16 * 256, 128),
        obs_prior.reshape(16 * 64, 128),
        obs_value,
        obs_prec,
        tile_batches.T,
        tile_count.reshape(1, 64),
        loc_weight.T,
    )
    return jnp.transpose(out, (1, 0, 2)).reshape(16, 64, 4, 128)


def solution(mesh):
    in_specs = (
        P("mem", "tile", None, None),
        P("mem", "tile", None),
        P("tile", None),
        P("tile", None),
        P("tile", None),
        P("tile"),
        P("tile", None),
    )
    out_specs = P("mem", "tile", None, None)
    return jax.shard_map(
        per_device, mesh=mesh, in_specs=in_specs, out_specs=out_specs, check_vma=False
    )
```

time: 113 us -> 104 us (0.920)
  the two profiles are of different devices: /device:TPU:2 before, /device:TPU:6 now
where the time goes in v2:
time: 104 us
  Pallas kernels  100 us (96%)
  local copies, waits for them, and re-layouts  3.72 us (4%)
    pallas_call x1, Pallas kernels, per_device(): pl.pallas_call(kernel, out_shape=jax.ShapeDtypeStruct((256, 16, 128), F32...  100 us
    reshape x1, local copies, waits for them, and re-layouts, per_device(): return jnp.transpose(out, (1, 0, 2)).reshape(16, 64, 4, 128)  3.72 us

profile of v2, /device:TPU:6, one launch (start us, length us, event | category | flops | bytes accessed | tf_op | source)
XLA Modules:
  0.0 104.0 jit_solution(17421775179329176585)
XLA Ops:
  0.0 100.2 %etkf.1 = f32[256,16,128]{2,1,0:T(8,128)} custom-call(f32[4096,128]{1,0:T(8,128)} %bitcast.9, f32[1024,128]{1,0:T(8,128)} %bitcast.10, f32[64,128]{1,0:T(8,128)} %val_hbm.1, f32[64,128]{1,0:T(8,128)} %prec_hbm.1, s32[6,64]{1,0:T(8,128)} %bitcast.11, s32[1,64]{1,0:T(1,128)} %bitcast.13, f32[6,64]{1,0:T(8,128)} %bitcast.12), custom_call_target="tpu_custom_call" | custom-call | tf_op jit(solution)/shard_map/etkf/pallas_call | solution.py:335
  100.2 3.7 %copy.8 = f32[16,64,4,128]{3,2,1,0:T(4,128)} copy(f32[16,64,4,128]{3,0,2,1:T(8,128)} %bitcast.8) | data formatting | bytes 4194304 | tf_op jit(solution)/shard_map/reshape | solution.py:385

commit v3 on v2

--- a/solution.py
+++ b/solution.py
@@ -12,6 +12,7 @@
 WINDOW = 36
 STEP = 1
 OSTEP = 1
+TURNS = 2
 GROUPS = ((0, 2), (2, 2), (4, 1), (5, 1), (6, 2), (8, 2))
 ORDER = (2, 3, 1, 4, 0, 5)
 
@@ -149,13 +150,11 @@
         auxes.append(remote(hbm, buf.at[q + 1], aux_send.at[n, 0], aux_recv.at[n, q + 1], sib))
         for core in range(2):
             auxes.append(remote(hbm, buf.at[3 - 3 * q], aux_send.at[n, 1 + core], aux_recv.at[n, 3 - 3 * q], (m, far + core)))
-    for copy in own_tabs + tabs + owns + auxes:
-        copy.start()
 
     def ob_group(n, k):
         w, size = GROUPS[n]
         core = w // 5
-        kk = lax.rem(k + m, 8)
+        kk = lax.rem(k + m + 2, 8)
         gd = lax.rem(8 * i + kk + 2 - w // 2 + 256, 256)
         md, td = lax.rem(gd, 16), 2 * (gd // 16) + core
         src = ob_t.at[pl.ds(4 * (2 * kk + w % 2), 4 * size)]
@@ -194,7 +193,11 @@
 
         lax.fori_loop(0, count, body, 0)
 
-    for n in ORDER:
+    for n in ORDER[:2]:
+        each(8, lambda k: launch(ob_group(n, k)))
+    for copy in own_tabs + tabs + owns + auxes:
+        copy.start()
+    for n in ORDER[2:]:
         each(8, lambda k: launch(ob_group(n, k)))
 
     load_st.wait()
@@ -207,7 +210,7 @@
     lax.fori_loop(0, 32, turn_st, 0)
 
     def st_unit(t, j):
-        kk, core = lax.rem(j // 2 + m, 8), lax.rem(j, 2)
+        kk, core = lax.rem(j // 2 + m + 2, 8), lax.rem(j, 2)
         md, td = 8 * q + kk, 2 * z + core
         src = st_t.at[pl.ds(16 * (2 * kk + core) + 4 * STEP * t, 4 * STEP)]
         dst = xbuf.at[pl.ds(4 * STEP * t, 4 * STEP), pl.ds(pl.multiple_of(16 * m, 16), 16)]
@@ -301,7 +304,7 @@
         return c
 
     def out_unit(t, j):
-        md = lax.rem(j + m, 16)
+        md = lax.rem(j + m + 10, 16)
         row = 4 * (8 * lax.rem(g, 8) + 4 * q + OSTEP * t)
         src = obuf.at[pl.ds(4 * OSTEP * t, 4 * OSTEP), pl.ds(pl.multiple_of(16 * md, 16), 16)]
         dst = out_ref.at[pl.ds(row, 4 * OSTEP)]
@@ -327,6 +330,11 @@
     for t in range(PER // OSTEP):
         each(16, lambda j: left(out_unit(t, j)))
     pltpu.make_async_copy(out_ref, out_ref, out_recv.at[0]).wait()
+
+
+def turn_kernel(in_ref, out_ref):
+    for k in range(16):
+        out_ref[k] = in_ref[pl.ds(k, 256 // TURNS, stride=16), :]
 
 
 def per_device(state, obs_prior, obs_value, obs_prec, tile_batches, tile_count, loc_weight):
@@ -382,7 +390,16 @@
         tile_count.reshape(1, 64),
         loc_weight.T,
     )
-    return jnp.transpose(out, (1, 0, 2)).reshape(16, 64, 4, 128)
+    turned = pl.pallas_call(
+        turn_kernel,
+        grid=(TURNS,),
+        out_shape=jax.ShapeDtypeStruct((16, 256, 128), F32),
+        in_specs=[pl.BlockSpec((16 * 256 // TURNS, 128), lambda b: (b, 0))],
+        out_specs=pl.BlockSpec((16, 256 // TURNS, 128), lambda b: (0, b, 0)),
+        compiler_params=pltpu.CompilerParams(vmem_limit_bytes=60 * 2**20),
+        name="turn",
+    )(out.reshape(256 * 16, 128))
+    return turned.reshape(16, 64, 4, 128)
 
 
 def solution(mesh):

time: 104 us -> 101 us (0.971); the launches traced: 104 us -> 99.4 us
  local copies, waits for them, and re-layouts: 3.72 us -> 0 us
    pallas_call x1, Pallas kernels: 100 us -> 96.4 us  [per_device(): pl.pallas_call(kernel, out_shape=jax.ShapeDtypeStruct((256, 16, 128), F32...]
    reshape x1 -> x0, local copies, waits for them, and re-layouts: 3.72 us -> none  [per_device(): return jnp.transpose(out, (1, 0, 2)).reshape(16, 64, 4, 128)]
    pallas_call x0 -> x1, Pallas kernels: none -> 2.91 us  [per_device(): pl.pallas_call(turn_kernel, grid=(TURNS,), out_shape=jax.ShapeDtypeStruct...]
where the time goes in v3:
time: 101 us; the launch traced here: 99.4 us
  Pallas kernels  99.3 us (98%)
    pallas_call x1, Pallas kernels, per_device(): pl.pallas_call(kernel, out_shape=jax.ShapeDtypeStruct((256, 16, 128), F32...  96.4 us
    pallas_call x1, Pallas kernels, per_device(): pl.pallas_call(turn_kernel, grid=(TURNS,), out_shape=jax.ShapeDtypeStruct...  2.91 us

profile of v3, /device:TPU:6, one launch (start us, length us, event | category | flops | bytes accessed | tf_op | source)
XLA Modules:
  0.0 99.4 jit_solution(8199537810554234608)
XLA Ops:
  0.0 96.4 %etkf.1 = f32[256,16,128]{2,1,0:T(8,128)} custom-call(f32[4096,128]{1,0:T(8,128)} %bitcast.8, f32[1024,128]{1,0:T(8,128)} %bitcast.9, f32[64,128]{1,0:T(8,128)} %val_hbm.1, f32[64,128]{1,0:T(8,128)} %prec_hbm.1, s32[6,64]{1,0:T(8,128)} %bitcast.10, s32[1,64]{1,0:T(1,128)} %bitcast.12, f32[6,64]{1,0:T(8,128)} %bitcast.11), custom_call_target="tpu_custom_call" | custom-call | tf_op jit(solution)/shard_map/etkf/pallas_call | solution.py:343
  96.4 2.9 %turn.1 = f32[16,256,128]{2,1,0:T(8,128)} custom-call(f32[4096,128]{1,0:T(8,128)} %bitcast.7), custom_call_target="tpu_custom_call" | custom-call | tf_op jit(solution)/shard_map/turn/pallas_call | solution.py:393

commit v4 on v3

--- a/solution.py
+++ b/solution.py
@@ -304,7 +304,7 @@
         return c
 
     def out_unit(t, j):
-        md = lax.rem(j + m + 10, 16)
+        md = lax.rem(j + m + 5, 16)
         row = 4 * (8 * lax.rem(g, 8) + 4 * q + OSTEP * t)
         src = obuf.at[pl.ds(4 * OSTEP * t, 4 * OSTEP), pl.ds(pl.multiple_of(16 * md, 16), 16)]
         dst = out_ref.at[pl.ds(row, 4 * OSTEP)]

time: 101 us -> 101 us (level)
  no operation moved by 1% of the time
where the time goes in v4:
time: 101 us; the launch traced here: 100 us
  Pallas kernels  100 us (99%)
    pallas_call x1, Pallas kernels, per_device(): pl.pallas_call(kernel, out_shape=jax.ShapeDtypeStruct((256, 16, 128), F32...  97.2 us
    pallas_call x1, Pallas kernels, per_device(): pl.pallas_call(turn_kernel, grid=(TURNS,), out_shape=jax.ShapeDtypeStruct...  2.91 us

profile of v4, /device:TPU:6, one launch (start us, length us, event | category | flops | bytes accessed | tf_op | source)
XLA Modules:
  0.0 100.1 jit_solution(12604084450609591111)
XLA Ops:
  0.0 97.2 %etkf.1 = f32[256,16,128]{2,1,0:T(8,128)} custom-call(f32[4096,128]{1,0:T(8,128)} %bitcast.8, f32[1024,128]{1,0:T(8,128)} %bitcast.9, f32[64,128]{1,0:T(8,128)} %val_hbm.1, f32[64,128]{1,0:T(8,128)} %prec_hbm.1, s32[6,64]{1,0:T(8,128)} %bitcast.10, s32[1,64]{1,0:T(1,128)} %bitcast.12, f32[6,64]{1,0:T(8,128)} %bitcast.11), custom_call_target="tpu_custom_call" | custom-call | tf_op jit(solution)/shard_map/etkf/pallas_call | solution.py:343
  97.2 2.9 %turn.1 = f32[16,256,128]{2,1,0:T(8,128)} custom-call(f32[4096,128]{1,0:T(8,128)} %bitcast.7), custom_call_target="tpu_custom_call" | custom-call | tf_op jit(solution)/shard_map/turn/pallas_call | solution.py:393

commit v5 on v4

--- a/solution.py
+++ b/solution.py
@@ -304,7 +304,7 @@
         return c
 
     def out_unit(t, j):
-        md = lax.rem(j + m + 5, 16)
+        md = lax.rem(m + 32 + (1 - 2 * q) * (j + 5), 16)
         row = 4 * (8 * lax.rem(g, 8) + 4 * q + OSTEP * t)
         src = obuf.at[pl.ds(4 * OSTEP * t, 4 * OSTEP), pl.ds(pl.multiple_of(16 * md, 16), 16)]
         dst = out_ref.at[pl.ds(row, 4 * OSTEP)]

time: 101 us -> 101 us (level)
  no operation moved by 1% of the time
where the time goes in v5:
time: 101 us; the launch traced here: 100 us
  Pallas kernels  100 us (99%)
    pallas_call x1, Pallas kernels, per_device(): pl.pallas_call(kernel, out_shape=jax.ShapeDtypeStruct((256, 16, 128), F32...  97.4 us
    pallas_call x1, Pallas kernels, per_device(): pl.pallas_call(turn_kernel, grid=(TURNS,), out_shape=jax.ShapeDtypeStruct...  2.91 us

profile of v5, /device:TPU:6, one launch (start us, length us, event | category | flops | bytes accessed | tf_op | source)
XLA Modules:
  0.0 100.3 jit_solution(4484942478967293863)
XLA Ops:
  0.0 97.4 %etkf.1 = f32[256,16,128]{2,1,0:T(8,128)} custom-call(f32[4096,128]{1,0:T(8,128)} %bitcast.8, f32[1024,128]{1,0:T(8,128)} %bitcast.9, f32[64,128]{1,0:T(8,128)} %val_hbm.1, f32[64,128]{1,0:T(8,128)} %prec_hbm.1, s32[6,64]{1,0:T(8,128)} %bitcast.10, s32[1,64]{1,0:T(1,128)} %bitcast.12, f32[6,64]{1,0:T(8,128)} %bitcast.11), custom_call_target="tpu_custom_call" | custom-call | tf_op jit(solution)/shard_map/etkf/pallas_call | solution.py:343
  97.4 2.9 %turn.1 = f32[16,256,128]{2,1,0:T(8,128)} custom-call(f32[4096,128]{1,0:T(8,128)} %bitcast.7), custom_call_target="tpu_custom_call" | custom-call | tf_op jit(solution)/shard_map/turn/pallas_call | solution.py:393
